TPU v7x, 512 devices: a whole 4x8x8 slice. The times are simulated.
512 devices in a mesh: party: 2 (over core), head: 16 (over z, y_lo), seq: 16 (over y_hi, x).
Axes of the slice: x: 4, y: 8 (y_hi: 4, y_lo: 2; y = y_hi * 2 + y_lo), z: 8, core: 2. Of those that a mesh axis runs over, the one named last changes fastest.
Arguments:
- query_share: bfloat16 [2, 32, 2048, 128], P('party', 'head', 'seq'), may hold values from -6 to 6
- key_share: bfloat16 [2, 32, 2048, 128], P('party', 'head', 'seq'), may hold values from -6 to 6
- value_share: bfloat16 [2, 32, 2048, 128], P('party', 'head', 'seq'), may hold values from -6 to 6
- query_mask: bfloat16 [2, 32, 2048, 128], P('party', 'head', 'seq'), may hold values from -6 to 6
- key_mask: bfloat16 [2, 32, 2048, 128], P('party', 'head', 'seq'), may hold values from -6 to 6
- value_mask: bfloat16 [2, 32, 2048, 128], P('party', 'head', 'seq'), may hold values from -1.5 to 1.5
- score_triple: bfloat16 [2, 32, 2048, 2048], P('party', 'head', 'seq'), may hold values from -6 to 6
- square_triple: bfloat16 [2, 32, 2048, 2048], P('party', 'head', 'seq'), may hold values from -6 to 6
- weight_mask: bfloat16 [2, 32, 2048, 2048], P('party', 'head', 'seq'), may hold values from -0.75 to 0.75
- output_triple: bfloat16 [2, 32, 2048, 128], P('party', 'head', 'seq'), may hold values from -3 to 3
- out_weight: bfloat16 [4096, 2560], P('head'), may hold values from -0.125 to 0.125
Outputs:
- mixed_share: float32 [2, 2048, 2560], P('party', 'seq', 'head')
All inputs are finite; a program needn't handle non-finite values.
Results may differ from a plain program's by a relative error of at most 0.0003.
Values may be sent and summed in bfloat16 or wider, within the bound.
A program may use at most 64 MiB of HBM per device.

v0:
```python
import jax
import jax.numpy as jnp
from jax import lax
from jax.sharding import PartitionSpec as P


def partner(value, axis, bit):
    mask = 2**bit
    pairs = [(source, source ^ mask) for source in range(lax.axis_size(axis))]
    return lax.ppermute(value, axis, pairs)


def pair_scores(left, right):
    return jnp.einsum("hqd,hkd->hqk", left, right, precision=lax.Precision.HIGHEST)


def apply_keys(weights, values):
    return jnp.einsum("hqk,hkd->hqd", weights, values, precision=lax.Precision.HIGHEST)


def body(
    query_share,
    key_share,
    value_share,
    query_mask,
    key_mask,
    value_mask,
    score_triple,
    square_triple,
    weight_mask,
    output_triple,
    out_weight,
):
    leader = (lax.axis_index("party") == 0).astype(jnp.float32)
    query_masked = query_mask[0].astype(jnp.float32)
    query_diff = query_share[0].astype(jnp.float32) - query_masked
    key_diff = key_share[0].astype(jnp.float32) - key_mask[0].astype(jnp.float32)
    value_diff = value_share[0].astype(jnp.float32) - value_mask[0].astype(jnp.float32)
    other_query, other_keys, other_values = partner((query_diff, key_diff, value_diff), "party", 0)
    opened_query = query_diff + other_query
    opened_keys, opened_values = (
        lax.all_gather(key_diff + other_keys, "seq", axis=1, tiled=True),
        lax.all_gather(value_diff + other_values, "seq", axis=1, tiled=True),
    )
    mask_keys, mask_values = (
        lax.all_gather(key_mask[0], "seq", axis=1, tiled=True),
        lax.all_gather(value_mask[0], "seq", axis=1, tiled=True),
    )
    scale_factor = query_diff.shape[-1] ** (-0.5)
    mask_keys_wide = mask_keys.astype(jnp.float32)
    score_part = scale_factor * (
        pair_scores(opened_query, mask_keys_wide + leader * opened_keys)
        + pair_scores(query_masked, opened_keys)
    )
    opened_scores = score_part + partner(score_part, "party", 0)
    triple_here = score_triple[0].astype(jnp.float32)
    share_scores = triple_here + score_part
    square_part = (
        square_triple[0].astype(jnp.float32)
        + 2.0 * opened_scores * triple_here
        + leader * opened_scores * opened_scores
    )
    poly = leader * 1.25 + share_scores + 0.25 * square_part
    tokens_here = score_part.shape[1]
    length = score_part.shape[2]
    rows = lax.axis_index("seq") * tokens_here + lax.broadcasted_iota(
        jnp.int32, (tokens_here, length), 0
    )
    cols = lax.broadcasted_iota(jnp.int32, (tokens_here, length), 1)
    row_scale = lax.rsqrt((rows + 1).astype(jnp.float32))
    weights = jnp.where(cols <= rows, poly * row_scale, 0.0)
    weight_here = weight_mask[0].astype(jnp.float32)
    weight_diff = weights - weight_here
    opened_weights = weight_diff + partner(weight_diff, "party", 0)
    values_all = mask_values.astype(jnp.float32) + leader * opened_values
    head_output = (
        output_triple[0].astype(jnp.float32)
        + apply_keys(opened_weights, values_all)
        + apply_keys(weight_here, opened_values)
    )
    heads_here = head_output.shape[0]
    weight_local = out_weight.astype(jnp.float32).reshape(
        heads_here, head_output.shape[2], out_weight.shape[1]
    )
    partial_value = jnp.einsum(
        "hqd,hdo->qo", head_output, weight_local, precision=lax.Precision.HIGHEST
    )
    total = lax.psum(partial_value, "head")
    width = total.shape[1] // lax.axis_size("head")
    result = lax.dynamic_slice_in_dim(total, lax.axis_index("head") * width, width, 1)
    return result[None]


def solution(mesh):
    in_specs = (
        P("party", "head", "seq", None),
        P("party", "head", "seq", None),
        P("party", "head", "seq", None),
        P("party", "head", "seq", None),
        P("party", "head", "seq", None),
        P("party", "head", "seq", None),
        P("party", "head", "seq", None),
        P("party", "head", "seq", None),
        P("party", "head", "seq", None),
        P("party", "head", "seq", None),
        P("head", None),
    )
    out_specs = P("party", "seq", "head")
    return jax.shard_map(body, mesh=mesh, in_specs=in_specs, out_specs=out_specs, check_vma=False)
```

profile of v0, /device:TPU:1, one launch (start us, length us, event | category | flops | bytes accessed | tf_op | source)
XLA Modules:
  0.0 419.3 jit_solution(12829437922483678689)
XLA Ops:
  6.5 0.0 copy-start
  6.5 0.0 all-gather.7.cloned.1.call-start
  6.5 1.0 subtract_bitcast_fusion.1
  7.5 8.8 %collective-permute-start.1 = (f32[2,128,128]{2,1,0:T(8,128)S(1)}, f32[2,128,128]{2,1,0:T(8,128)S(1)}, u32[]{:S(2)}, u32[]{:S(2)}) collective-permute-start(f32[2,128,128]{2,1,0:T(8,128)S(1)} %subtract_bitcast_fusion.1), channel_id=1, source_target_pairs={{0,256},{256,0},{1,257},{257,1},{2,258},{258,2},{3,259},{259,3},{4... | collective-permute-start | bytes 393224 | tf_op jit(solution)/shard_map/ppermute | solution.py:10
  16.3 1.0 collective-permute-done.1
  17.3 1.6 fusion.26
  18.9 0.0 all-gather.7.cloned.1.call-update
  18.9 0.0 all-gather.11.cloned.1.call-start
  18.9 0.7 all-gather.11.cloned.1.call-update
  19.6 0.0 all-gather.9.cloned.1.call-start
  19.7 0.9 subtract_bitcast_fusion
  20.6 2.3 collective-permute-start.4
  22.8 1.0 collective-permute-done.4
  23.8 1.5 fusion.27
  25.4 0.0 all-gather.9.cloned.1.call-update
  25.4 0.0 all-gather.13.cloned.1.call-start
  25.4 0.9 convert_subtract_fusion
  26.3 2.3 collective-permute-start
  28.6 0.0 copy-start.2
  28.6 0.0 copy-start.3
  28.6 53.6 %all-gather.7.cloned.1.call-done = f32[2,2048,128]{2,1,0:T(8,128)} async-done(((f32[2,128,128]{2,1,0:T(8,128)}), f32[2,2048,128]{2,1,0:T(8,128)}) %all-gather.7.cloned.1.call-update) | async-done | bytes 2097168 | tf_op jit(solution)/shard_map/all_gather | solution.py:42
  82.3 4.1 convolution_bitcast_fusion.1
  86.4 0.0 collective-permute-done
  86.4 0.0 copy-start.4
  86.4 0.6 copy-done.4
  87.1 53.8 %all-gather.11.cloned.1.call-done = bf16[1,2,2048,128]{3,2,1,0:T(8,128)(2,1)} async-done(((bf16[1,2,128,128]{3,2,1,0:T(8,128)(2,1)}), bf16[1,2,2048,128]{3,2,1,0:T(8,128)(2,1)}) %all-gather.11.cloned.1.call-update) | async-done | bytes 1048592 | tf_op jit(solution)/shard_map/all_gather | solution.py:46
  140.9 0.0 copy-done.2
  140.9 0.0 copy-done.3
  140.9 4.6 %fusion = f32[2,128,2048]{2,1,0:T(8,128)S(1)} fusion(f32[2,128,2048]{2,1,0:T(8,128)} %convolution_bitcast_fusion.1, f32[2,2048,128]{2,1,0:T(8,128)} %all-gather.7.cloned.1.call-done, bf16[1,2,2048,128]{3,2,1,0:T(8,128)(2,1)} %all-gather.11.cloned.1.call-done, f32[]{:T(128)S(6)} %convert_element_type.71, f32[2,128,128]{2,1,0:T(8,128)} %copy-done.4, ...), kind=kOutput, calls=%fused_computation.4 | convolution fusion | flops 808058880 | bytes 7602180 | tf_op jit(solution)/shard_map/hqd,hkd->hqk/dot_general | solution.py:14
  145.5 0.0 copy-start.1
  145.5 3.4 collective-permute-start.2
  149.0 0.2 iota_compare_fusion
  149.2 0.0 copy-done.1
  149.2 3.6 collective-permute-done.2
  152.8 4.4 %fusion.5 = f32[2,128,2048]{2,1,0:T(8,128)S(1)} fusion(f32[2,128,2048]{2,1,0:T(8,128)} %copy-done.1, f32[2,128,2048]{2,1,0:T(8,128)} %collective-permute-done.2, bf16[1,2,128,2048]{3,2,1,0:T(8,128)(2,1)} %param.18, bf16[1,2,128,2048]{3,2,1,0:T(8,128)(2,1)} %param.19, bf16[1,2,128,2048]{3,2,1,0:T(8,128)(2,1)} %param.17, f32[128]{0:T(128)S(1)} %convert_rsqrt_fusion, ...), kind=kLoop, calls=%fused_computation.11 | loop fusion | flops 8912896 | bytes 9699848 | tf_op jit(solution)/shard_map/sub | solution.py:73
  157.2 2.3 collective-permute-start.3
  159.5 0.0 all-gather.13.cloned.1.call-update
  159.5 0.0 all-reduce.2.cloned.1.call-start
  159.6 46.9 %all-gather.9.cloned.1.call-done = f32[2,2048,128]{2,1,0:T(8,128)} async-done(((f32[2,128,128]{2,1,0:T(8,128)}), f32[2,2048,128]{2,1,0:T(8,128)}) %all-gather.9.cloned.1.call-update) | async-done | bytes 2097168 | tf_op jit(solution)/shard_map/all_gather | solution.py:43
  206.4 3.1 convolution_bitcast_fusion.2
  209.5 55.4 %all-gather.13.cloned.1.call-done = bf16[1,2,2048,128]{3,2,1,0:T(8,128)(2,1)} async-done(((bf16[1,2,128,128]{3,2,1,0:T(8,128)(2,1)}), bf16[1,2,2048,128]{3,2,1,0:T(8,128)(2,1)}) %all-gather.13.cloned.1.call-update) | async-done | bytes 1048592 | tf_op jit(solution)/shard_map/all_gather | solution.py:47
  264.9 0.0 collective-permute-done.3
  264.9 4.9 %fusion.16 = f32[2,128,128]{2,1,0:T(8,128)S(1)} fusion(f32[2,128,128]{2,1,0:T(8,128)S(1)} %convolution_bitcast_fusion.2, f32[2,2048,128]{2,1,0:T(8,128)} %all-gather.9.cloned.1.call-done, f32[2,128,2048]{2,1,0:T(8,128)S(1)} %fusion.5, f32[2,128,2048]{2,1,0:T(8,128)} %collective-permute-done.3, bf16[1,2,2048,128]{3,2,1,0:T(8,128)(2,1)} %all-gather.13.cloned.1.call-done, ...), kind=kOutput, calls=%fused_computation.23 | convolution fusion | flops 807501824 | bytes 7667716 | tf_op jit(solution)/shard_map/hqk,hkd->hqd/dot_general | solution.py:18
  269.8 0.0 copy-done
  269.8 2.5 convolution_bitcast_fusion
  272.4 0.0 all-reduce.2.cloned.1.call-update
  272.4 138.9 %all-reduce.2.cloned.1.call-done = f32[128,2560]{0,1:T(8,128)} async-done(((f32[128,2560]{0,1:T(8,128)}), f32[128,2560]{0,1:T(8,128)}) %all-reduce.2.cloned.1.call-update) | async-done | bytes 1310736 | tf_op jit(solution)/shard_map/psum | solution.py:88
  411.3 1.5 dynamic-slice_bitcast_fusion
  (2 shorter events, 0.0 us)
Async XLA Ops:
  6.5 263.3 %copy-start = (bf16[256,2560]{1,0:T(8,128)(2,1)S(1)}, bf16[256,2560]{1,0:T(8,128)(2,1)}, u32[]{:S(2)}) copy-start(bf16[256,2560]{1,0:T(8,128)(2,1)} %param.21) | copy-start | bytes 3932164
  6.5 75.7 %all-gather.7.cloned.1.call-start = ((), (), s32[]{:S(2)}) async-start(), calls=%async_computation | async-start | bytes 2228224 | tf_op jit(solution)/shard_map/all_gather | solution.py:42
  7.5 9.8 %collective-permute-start.1 = (f32[2,128,128]{2,1,0:T(8,128)S(1)}, f32[2,128,128]{2,1,0:T(8,128)S(1)}, u32[]{:S(2)}, u32[]{:S(2)}) collective-permute-start(f32[2,128,128]{2,1,0:T(8,128)S(1)} %subtract_bitcast_fusion.1), channel_id=1, source_target_pairs={{0,256},{256,0},{1,257},{257,1},{2,258},{258,2},{3,259},{259,3},{4... | collective-permute-start | bytes 393224 | tf_op jit(solution)/shard_map/ppermute | solution.py:10
  18.9 122.0 %all-gather.11.cloned.1.call-start = ((), (), s32[]{:S(2)}) async-start(), calls=%async_computation.3 | async-start | bytes 1114112 | tf_op jit(solution)/shard_map/all_gather | solution.py:46
  19.6 186.8 %all-gather.9.cloned.1.call-start = ((), (), s32[]{:S(2)}) async-start(), calls=%async_computation.1 | async-start | bytes 2228224 | tf_op jit(solution)/shard_map/all_gather | solution.py:43
  20.6 3.2 collective-permute-start.4
  25.4 239.5 %all-gather.13.cloned.1.call-start = ((), (), s32[]{:S(2)}) async-start(), calls=%async_computation.4 | async-start | bytes 1114112 | tf_op jit(solution)/shard_map/all_gather | solution.py:47
  26.3 60.1 %collective-permute-start = (f32[2,128,128]{2,1,0:T(8,128)S(1)}, f32[2,128,128]{2,1,0:T(8,128)S(1)}, u32[]{:S(2)}, u32[]{:S(2)}) collective-permute-start(f32[2,128,128]{2,1,0:T(8,128)S(1)} %convert_subtract_fusion), channel_id=1, source_target_pairs={{0,256},{256,0},{1,257},{257,1},{2,258},{258,2},{3,259},{259,3},{4... | collective-permute-start | bytes 393224 | tf_op jit(solution)/shard_map/ppermute | solution.py:10
  28.6 112.3 %copy-start.2 = (bf16[1,2,128,128]{3,2,1,0:T(8,128)(2,1)S(1)}, bf16[1,2,128,128]{3,2,1,0:T(8,128)(2,1)}, u32[]{:S(2)}) copy-start(bf16[1,2,128,128]{3,2,1,0:T(8,128)(2,1)} %param.14) | copy-start | bytes 196612
  28.6 112.3 %copy-start.3 = (bf16[1,2,128,128]{3,2,1,0:T(8,128)(2,1)S(1)}, bf16[1,2,128,128]{3,2,1,0:T(8,128)(2,1)}, u32[]{:S(2)}) copy-start(bf16[1,2,128,128]{3,2,1,0:T(8,128)(2,1)} %param.11) | copy-start | bytes 196612
  86.4 0.6 copy-start.4
  145.5 3.7 copy-start.1
  145.5 7.3 %collective-permute-start.2 = (f32[2,128,2048]{2,1,0:T(8,128)S(1)}, f32[2,128,2048]{2,1,0:T(8,128)}, u32[]{:S(2)}, u32[]{:S(2)}) collective-permute-start(f32[2,128,2048]{2,1,0:T(8,128)S(1)} %fusion), channel_id=1, source_target_pairs={{0,256},{256,0},{1,257},{257,1},{2,258},{258,2},{3,259},{259,3},{4... | collective-permute-start | bytes 6291464 | tf_op jit(solution)/shard_map/ppermute | solution.py:10
  157.2 107.7 %collective-permute-start.3 = (f32[2,128,2048]{2,1,0:T(8,128)S(1)}, f32[2,128,2048]{2,1,0:T(8,128)}, u32[]{:S(2)}, u32[]{:S(2)}) collective-permute-start(f32[2,128,2048]{2,1,0:T(8,128)S(1)} %fusion.5), channel_id=1, source_target_pairs={{0,256},{256,0},{1,257},{257,1},{2,258},{258,2},{3,259},{259,3},{4... | collective-permute-start | bytes 6291464 | tf_op jit(solution)/shard_map/ppermute | solution.py:10
  159.5 251.7 %all-reduce.2.cloned.1.call-start = ((), (), s32[]{:S(2)}) async-start(), calls=%async_computation.2 | async-start | bytes 2621440 | tf_op jit(solution)/shard_map/psum | solution.py:88
Sparse Core Ops, SparseCore 0:
  19.0 63.2 all-gather.6
  85.3 55.5 all-gather.10
  143.9 62.4 all-gather.8
  209.3 55.5 all-gather.12
  272.5 138.7 all-reduce.1
where the time goes:
time: 428 us; the launch traced here: 419 us
  waiting for transfers between devices  355 us (83%)
  matrix products  19.3 us (5%)
  starting transfers between devices  19.2 us (4%)
  between operations  13.3 us (3%)
  other arithmetic  10.5 us (2%)
    psum x1, waiting for transfers between devices, body(): total = lax.psum(partial_value, 'head')  139 us
    all_gather x1, waiting for transfers between devices, body(): lax.all_gather(value_mask[0], 'seq', axis=1, tiled=True)  55.4 us
    all_gather x1, waiting for transfers between devices, body(): lax.all_gather(key_mask[0], 'seq', axis=1, tiled=True)  53.8 us
    all_gather x1, waiting for transfers between devices, body(): lax.all_gather(key_diff + other_keys, 'seq', axis=1, tiled=True)  53.6 us
    all_gather x1, waiting for transfers between devices, body(): lax.all_gather(value_diff + other_values, 'seq', axis=1, tiled=True)  46.9 us
    ppermute x5, starting transfers between devices, partner(): return lax.ppermute(value, axis, pairs)  19 us
    dot_general x2, matrix products, pair_scores(): jnp.einsum('hqd,hkd->hqk', left, right, precision=lax.Precision.HIGHEST)  8.76 us
  transfers between devices with their start and end apart: 10, of which 8 were waited for; matrix products, arithmetic and copies ran while one was open for 5% of the time, Pallas kernels for 0%

commit v1 on v0

v1 whole, which is shorter than its diff:
```python
import functools

import jax
import jax.numpy as jnp
from jax import lax
from jax.experimental import pallas as pl
from jax.experimental.pallas import tpu as pltpu
from jax.sharding import PartitionSpec as P

F32 = jnp.float32
BF16 = jnp.bfloat16
T = 128
NX, NY, NZ = 4, 4, 8
SLOTS = NX * NY
COLS = 160
CHUNKS = ((0, 3, True, 1), (3, 3, True, -1), (6, 1, False, 1), (7, 1, False, -1))
SUBS = 2
ROWS = COLS // SUBS


def split(value):
    high = value.astype(BF16)
    return high, (value - high.astype(F32)).astype(BF16)


def nt(left, right):
    return lax.dot_general(left, right, (((1,), (1,)), ((), ())), preferred_element_type=F32)


def nn(left, right):
    return lax.dot_general(left, right, (((1,), (0,)), ((), ())), preferred_element_type=F32)


def kernel(
    ks, km, vs, vm, qs, qm, ot, zt, st, wm, ow, out_ref,
    kv, qo, big, wt_in, wt, gat, qa, acc, outs, pt, rsb, fin, fin_rx,
    loc_sem, swp_send, swp_recv, w_sem, g_send, g_recv, h_send, h_recv, r_send, r_recv, y_send, y_recv,
):
    party = lax.axis_index("party")
    head = lax.axis_index("head")
    seq = lax.axis_index("seq")
    z, ylo = head // 2, head % 2
    yh, x = seq // NX, seq % NX
    sib = {"party": 1 - party}

    def at_slot(y, xx):
        return (y % NY) * NX + xx % NX

    def at_z(zz):
        return {"head": (zz % NZ) * 2 + ylo}

    peers = [
        sib,
        {"seq": at_slot(yh, x + 1)},
        {"seq": at_slot(yh, x + NX - 1)},
        {"seq": at_slot(yh + 1, x)},
        {"seq": at_slot(yh + NY - 1, x)},
        at_z(z + 1),
        at_z(z + NZ - 1),
        {"head": z * 2 + 1 - ylo},
    ]
    barrier = pltpu.get_barrier_semaphore()
    for peer in peers:
        pl.semaphore_signal(barrier, inc=1, device_id=peer, device_id_type=pl.DeviceIdType.MESH)

    arrays = [ks, km, vs, vm, qs, qm, ot, zt, st, wm]
    places = [kv.at[i] for i in range(4)] + [qo.at[i] for i in range(3)] + [big.at[i] for i in range(3)]
    locals_ = []
    for i, (src, dst) in enumerate(zip(arrays, places)):
        locals_.append(pltpu.make_async_copy(src.at[0, party], dst.at[party], loc_sem.at[i]))
        locals_[-1].start()
    weights_in = pltpu.make_async_copy(ow, wt_in, w_sem)
    weights_in.start()
    pl.semaphore_wait(barrier, len(peers))
    swaps = []
    for i, (src, dst) in enumerate(zip(arrays, places)):
        swaps.append(
            pltpu.make_async_remote_copy(
                src_ref=src.at[0, 1 - party],
                dst_ref=dst.at[party],
                send_sem=swp_send.at[i],
                recv_sem=swp_recv.at[i],
                device_id=sib,
                device_id_type=pl.DeviceIdType.MESH,
            )
        )
        swaps[-1].start()

    def arrived(i):
        locals_[i].wait()
        swaps[i].wait_recv()

    for i in range(4):
        arrived(i)

    def wide(ref):
        return ref[...].astype(F32)

    kh, kl = split(wide(kv.at[0, 0]) + wide(kv.at[0, 1]))
    bh, bl = split(wide(kv.at[1, 0]) + wide(kv.at[1, 1]))
    dh, dl = split(
        (wide(kv.at[2, 0]) - wide(kv.at[3, 0])) + (wide(kv.at[2, 1]) - wide(kv.at[3, 1]))
    )
    for i, value in enumerate((kh, kl, bh, bl, dh, dl, kv[3, 0], kv[3, 1])):
        gat[seq, i] = value

    sends = []

    def copy(chunk, first, second, y, xx, target):
        start, count = CHUNKS[chunk][:2]
        place = gat.at[at_slot(y, xx), pl.ds(start, count)]
        return pltpu.make_async_remote_copy(
            src_ref=place,
            dst_ref=place,
            send_sem=g_send.at[chunk * 16 + first * 4 + second],
            recv_sem=g_recv.at[chunk * 16 + first * 4 + second],
            device_id={"seq": target},
            device_id_type=pl.DeviceIdType.MESH,
        )

    def send(chunk, first, second, y, xx, along_y, step):
        target = at_slot(yh + step + NY, x) if along_y else at_slot(yh, x + step + NX)
        one = copy(chunk, first, second, y, xx, target)
        one.start()
        sends.append(one)

    def origin(chunk, first, second):
        _, _, y_first, sign = CHUNKS[chunk]
        moves = (0, -sign, sign, 2)
        dy, dx = (moves[first], moves[second]) if y_first else (moves[second], moves[first])
        return yh + dy + NY, x + dx + NX

    def spread_second(chunk, first):
        _, _, y_first, sign = CHUNKS[chunk]
        y, xx = origin(chunk, first, 0)
        send(chunk, first, 1, y, xx, not y_first, sign)
        send(chunk, first, 2, y, xx, not y_first, -sign)

    def receive(chunk, first, second):
        _, _, y_first, sign = CHUNKS[chunk]
        y, xx = origin(chunk, first, second)
        copy(chunk, first, second, y, xx, seq).wait_recv()
        if second == 0:
            if first == 1:
                send(chunk, 3, 0, y, xx, y_first, sign)
            spread_second(chunk, first)
        elif second == 1:
            send(chunk, first, 3, y, xx, not y_first, sign)

    for chunk, (_, _, y_first, sign) in enumerate(CHUNKS):
        send(chunk, 1, 0, yh, x, y_first, sign)
        send(chunk, 2, 0, yh, x, y_first, -sign)
    for chunk in range(4):
        spread_second(chunk, 0)

    for i in range(4, 7):
        arrived(i)
    scale = T ** (-0.5)
    qh, ql = split(scale * (wide(qo.at[0, 0]) + wide(qo.at[0, 1])))
    ah, al = split(-scale * (wide(qo.at[1, 0]) + wide(qo.at[1, 1])))
    for i, value in enumerate((qh, qh, ql, ah, ah, al)):
        qa[:, i * T : (i + 1) * T] = value
    acc[0] = wide(qo.at[2, 0])
    acc[1] = wide(qo.at[2, 1])
    for i in range(7, 10):
        arrived(i)

    def attend(slot):
        cols = pl.ds(pl.multiple_of(slot * T, T), T)
        kh, kl, bh, bl, dh, dl, c0, c1 = [gat[slot, i] for i in range(8)]
        scores = nt(qa[...], jnp.concatenate([kh, kl, kh, bh, bl, bh], axis=1))
        zz = big[0, 0, :, cols].astype(F32) + big[0, 1, :, cols].astype(F32)
        sq = big[1, 0, :, cols].astype(F32) + big[1, 1, :, cols].astype(F32)
        w0 = big[2, 0, :, cols]
        w1 = big[2, 1, :, cols]
        poly = 1.25 + zz + 0.25 * sq + scores * (1.0 + 0.5 * zz + 0.25 * scores)
        row = seq * T + lax.broadcasted_iota(jnp.int32, (T, T), 0)
        col = slot * T + lax.broadcasted_iota(jnp.int32, (T, T), 1)
        weights = jnp.where(col <= row, poly * lax.rsqrt((row + 1).astype(F32)), 0.0)
        lead = weights - w1.astype(F32)
        opened = lead - w0.astype(F32)
        lh, ll = split(lead)
        oh, ol = split(opened)
        both = jnp.concatenate([c0, c1], axis=1)
        mixed = nn(jnp.concatenate([oh, ol], axis=1), jnp.concatenate([both, both], axis=0))
        acc[0] += mixed[:, :T] + nn(
            jnp.concatenate([lh, ll, lh], axis=1), jnp.concatenate([dh, dh, dl], axis=0)
        )
        acc[1] += mixed[:, T:] + nn(
            jnp.concatenate([w1, w1], axis=1), jnp.concatenate([dh, dl], axis=0)
        )

    def attend_at(dy, dx):
        attend(at_slot(yh + dy + NY, x + dx + NX))

    attend_at(0, 0)
    for chunk in range(4):
        receive(chunk, 1, 0)
    for chunk in range(4):
        receive(chunk, 2, 0)
    for chunk in range(4):
        receive(chunk, 0, 1)
    weights_in.wait()

    @pl.loop(0, 20)
    def _(i):
        cols = pl.ds(pl.multiple_of(i * T, T), T)
        wt[cols, :] = wt_in[:, cols].T

    for chunk in range(4):
        receive(chunk, 0, 2)
    for dy, dx in ((1, 0), (-1, 0), (0, 1), (0, -1)):
        attend_at(dy, dx)
    for chunk in range(4):
        receive(chunk, 3, 0)
    for chunk in range(4):
        receive(chunk, 1, 1)
        receive(chunk, 2, 1)
    for chunk in range(4):
        receive(chunk, 0, 3)
        receive(chunk, 1, 2)
        receive(chunk, 2, 2)
        receive(chunk, 3, 1)
    for dy, dx in ((2, 0), (0, 2), (1, 1), (1, -1), (-1, 1), (-1, -1)):
        attend_at(dy, dx)
    for chunk in range(4):
        receive(chunk, 3, 2)
        receive(chunk, 1, 3)
        receive(chunk, 2, 3)
    for dy, dx in ((2, 1), (2, -1), (1, 2), (-1, 2)):
        attend_at(dy, dx)
    for chunk in range(4):
        receive(chunk, 3, 3)
    attend_at(2, 2)

    swap = pltpu.make_async_remote_copy(
        src_ref=acc.at[1 - party],
        dst_ref=outs.at[party],
        send_sem=h_send,
        recv_sem=h_recv,
        device_id=sib,
        device_id_type=pl.DeviceIdType.MESH,
    )
    swap.start()
    outs[party] = acc[party]
    swap.wait_recv()
    oh, ol = split(jnp.concatenate([outs[0], outs[1]], axis=1))
    ohl = jnp.concatenate([oh, ol], axis=1)

    def project(zz):
        rows = pl.ds(pl.multiple_of((zz % NZ) * 2 * COLS, 2 * COLS), 2 * COLS)
        part = wt[rows, :]
        pt[zz % NZ] = nt(jnp.concatenate([part, part], axis=1), ohl)

    ring = []

    def ring_copy(way, step, sub, src):
        index = (way * (NZ - 1) + step) * SUBS + sub
        return pltpu.make_async_remote_copy(
            src_ref=src,
            dst_ref=rsb.at[way, step, pl.ds(sub * ROWS, ROWS)],
            send_sem=r_send.at[index],
            recv_sem=r_recv.at[index],
            device_id=at_z(z + 1) if way == 0 else at_z(z + NZ - 1),
            device_id_type=pl.DeviceIdType.MESH,
        )

    def block_of(way, step):
        return (z - 1 - step + 2 * NZ) % NZ if way == 0 else (z + 1 + step) % NZ

    def local(way, step, sub):
        return pt.at[block_of(way, step), pl.ds(way * COLS + sub * ROWS, ROWS)]

    project(z + NZ - 1)
    for sub in range(SUBS):
        ring.append(ring_copy(0, 0, sub, local(0, 0, sub)))
        ring[-1].start()
    project(z + 1)
    for sub in range(SUBS):
        ring.append(ring_copy(1, 0, sub, local(1, 0, sub)))
        ring[-1].start()
    for step in (2, 6, 3, 5, 4, 0):
        project(z + step)
    for step in range(1, NZ):
        for sub in range(SUBS):
            for way in range(2):
                index = ring_copy(way, step - 1, sub, local(way, 0, sub))
                index.wait_recv()
                place = rsb.at[way, step - 1, pl.ds(sub * ROWS, ROWS)]
                total = place[...] + local(way, step, sub)[...]
                if step < NZ - 1:
                    place[...] = total
                    ring.append(ring_copy(way, step, sub, place))
                    ring[-1].start()
                else:
                    fin[way, pl.ds(sub * ROWS, ROWS)] = total
    last = pltpu.make_async_remote_copy(
        src_ref=fin.at[1 - ylo],
        dst_ref=fin_rx,
        send_sem=y_send,
        recv_sem=y_recv,
        device_id={"head": z * 2 + 1 - ylo},
        device_id_type=pl.DeviceIdType.MESH,
    )
    last.start()
    last.wait_recv()
    out_ref[...] = fin[ylo] + fin_rx[...]
    for one in swaps + sends + [swap] + ring + [last]:
        one.wait_send()


def body(
    query_share, key_share, value_share, query_mask, key_mask, value_mask,
    score_triple, square_triple, weight_mask, output_triple, out_weight,
):
    dma = pltpu.SemaphoreType.DMA
    result = pl.pallas_call(
        kernel,
        out_shape=jax.ShapeDtypeStruct((COLS, T), F32),
        in_specs=[pl.BlockSpec(memory_space=pl.ANY)] * 11,
        out_specs=pl.BlockSpec(memory_space=pltpu.VMEM),
        scratch_shapes=[
            pltpu.VMEM((4, 2, T, T), BF16),
            pltpu.VMEM((3, 2, T, T), BF16),
            pltpu.VMEM((3, 2, T, SLOTS * T), BF16),
            pltpu.VMEM((2 * T, 16 * COLS), BF16),
            pltpu.VMEM((16 * COLS, 2 * T), BF16),
            pltpu.VMEM((SLOTS, 8, T, T), BF16),
            pltpu.VMEM((T, 6 * T), BF16),
            pltpu.VMEM((2, T, T), F32),
            pltpu.VMEM((2, T, T), F32),
            pltpu.VMEM((NZ, 2 * COLS, T), F32),
            pltpu.VMEM((2, NZ - 1, COLS, T), F32),
            pltpu.VMEM((2, COLS, T), F32),
            pltpu.VMEM((COLS, T), F32),
            dma((10,)),
            dma((10,)),
            dma((10,)),
            dma,
            dma((64,)),
            dma((64,)),
            dma,
            dma,
            dma((2 * (NZ - 1) * SUBS,)),
            dma((2 * (NZ - 1) * SUBS,)),
            dma,
            dma,
        ],
        compiler_params=pltpu.CompilerParams(
            collective_id=0, has_side_effects=True, vmem_limit_bytes=40 * 1024 * 1024
        ),
    )(
        key_share, key_mask, value_share, value_mask, query_share, query_mask, output_triple,
        score_triple, square_triple, weight_mask, out_weight,
    )
    return result.T[None]


def solution(mesh):
    shares = P("party", "head", "seq", None)
    return jax.shard_map(
        body,
        mesh=mesh,
        in_specs=(shares,) * 10 + (P("head", None),),
        out_specs=P("party", "seq", "head"),
        check_vma=False,
    )
```

time: 428 us -> 92.8 us (0.22)
  the two profiles are of different devices: /device:TPU:1 before, /device:TPU:8 now
where the time goes in v1:
time: 92.8 us; the launch traced here: 92.2 us
  Pallas kernels  80.7 us (87%)
  local copies, waits for them, and re-layouts  11.5 us (12%)
    pallas_call x1, Pallas kernels, body(): pl.pallas_call(kernel, out_shape=jax.ShapeDtypeStruct((COLS, T), F32), in...  80.7 us
    unnamed x23, local copies, waits for them, and re-layouts  11.5 us

profile of v1, /device:TPU:8, one launch (start us, length us, event | category | flops | bytes accessed | tf_op | source)
XLA Modules:
  0.0 92.2 jit_solution(3801400754069693083)
XLA Ops:
  0.0 0.0 copy-start
  0.0 1.3 %copy-done = bf16[256,2560]{1,0:T(8,128)(2,1)S(1)} copy-done((bf16[256,2560]{1,0:T(8,128)(2,1)S(1)}, bf16[256,2560]{1,0:T(8,128)(2,1)}, u32[]{:S(2)}) %copy-start) | copy-done | bytes 1310744
  1.3 0.0 copy-start.1
  1.3 1.2 %copy-done.1 = bf16[1,2,128,2048]{3,2,1,0:T(8,128)(2,1)S(1)} copy-done((bf16[1,2,128,2048]{3,2,1,0:T(8,128)(2,1)S(1)}, bf16[1,2,128,2048]{3,2,1,0:T(8,128)(2,1)}, u32[]{:S(2)}) %copy-start.1) | copy-done | bytes 1048600
  2.5 0.0 copy-start.2
  2.5 1.2 %copy-done.2 = bf16[1,2,128,2048]{3,2,1,0:T(8,128)(2,1)S(1)} copy-done((bf16[1,2,128,2048]{3,2,1,0:T(8,128)(2,1)S(1)}, bf16[1,2,128,2048]{3,2,1,0:T(8,128)(2,1)}, u32[]{:S(2)}) %copy-start.2) | copy-done | bytes 1048600
  3.8 0.0 copy-start.3
  3.8 1.2 %copy-done.3 = bf16[1,2,128,2048]{3,2,1,0:T(8,128)(2,1)S(1)} copy-done((bf16[1,2,128,2048]{3,2,1,0:T(8,128)(2,1)S(1)}, bf16[1,2,128,2048]{3,2,1,0:T(8,128)(2,1)}, u32[]{:S(2)}) %copy-start.3) | copy-done | bytes 1048600
  5.0 0.0 copy-start.4
  5.0 0.8 copy-done.4
  5.8 0.0 copy-start.5
  5.8 0.8 copy-done.5
  6.7 0.0 copy-start.6
  6.7 0.8 copy-done.6
  7.5 0.0 copy-start.7
  7.5 0.8 copy-done.7
  8.4 0.0 copy-start.8
  8.4 0.8 copy-done.8
  9.2 0.0 copy-start.9
  9.2 0.8 copy-done.9
  10.0 0.0 copy-start.10
  10.0 0.8 copy-done.10
  10.9 80.7 %shard_map.109 = f32[160,128]{1,0:T(8,128)S(1)} custom-call(bf16[1,2,128,128]{3,2,1,0:T(8,128)(2,1)S(1)} %copy-done.4, bf16[1,2,128,128]{3,2,1,0:T(8,128)(2,1)S(1)} %copy-done.5, bf16[1,2,128,128]{3,2,1,0:T(8,128)(2,1)S(1)} %copy-done.6, bf16[1,2,128,128]{3,2,1,0:T(8,128)(2,1)S(1)} %copy-done.7, bf16[1,2,128,128]{3,2,1,0:T(8,128)(2,1)S(1)} %copy-done.8, ...), custom_call_target="tpu_custom_call" | custom-call | tf_op jit(solution)/shard_map/pallas_call | solution.py:317
  91.6 0.6 copy.13
Async XLA Ops:
  0.0 1.3 %copy-start = (bf16[256,2560]{1,0:T(8,128)(2,1)S(1)}, bf16[256,2560]{1,0:T(8,128)(2,1)}, u32[]{:S(2)}) copy-start(bf16[256,2560]{1,0:T(8,128)(2,1)} %ow.1) | copy-start | bytes 3932164
  1.3 1.2 %copy-start.1 = (bf16[1,2,128,2048]{3,2,1,0:T(8,128)(2,1)S(1)}, bf16[1,2,128,2048]{3,2,1,0:T(8,128)(2,1)}, u32[]{:S(2)}) copy-start(bf16[1,2,128,2048]{3,2,1,0:T(8,128)(2,1)} %zt.1) | copy-start | bytes 3145732
  2.5 1.2 %copy-start.2 = (bf16[1,2,128,2048]{3,2,1,0:T(8,128)(2,1)S(1)}, bf16[1,2,128,2048]{3,2,1,0:T(8,128)(2,1)}, u32[]{:S(2)}) copy-start(bf16[1,2,128,2048]{3,2,1,0:T(8,128)(2,1)} %st.1) | copy-start | bytes 3145732
  3.8 1.2 %copy-start.3 = (bf16[1,2,128,2048]{3,2,1,0:T(8,128)(2,1)S(1)}, bf16[1,2,128,2048]{3,2,1,0:T(8,128)(2,1)}, u32[]{:S(2)}) copy-start(bf16[1,2,128,2048]{3,2,1,0:T(8,128)(2,1)} %wm.1) | copy-start | bytes 3145732
  5.0 0.8 copy-start.4
  5.8 0.8 copy-start.5
  6.7 0.8 copy-start.6
  7.5 0.8 copy-start.7
  8.4 0.8 copy-start.8
  9.2 0.8 copy-start.9
  10.0 0.8 copy-start.10

commit v2 on v1

--- a/solution.py
+++ b/solution.py
@@ -13,9 +13,12 @@
 NX, NY, NZ = 4, 4, 8
 SLOTS = NX * NY
 COLS = 160
-CHUNKS = ((0, 3, True, 1), (3, 3, True, -1), (6, 1, False, 1), (7, 1, False, -1))
-SUBS = 2
-ROWS = COLS // SUBS
+SCALES = 5 * T
+BLOCK = SCALES + 16
+CHUNKS = ((0, 256, True, 1), (256, 256, True, -1), (512, 80, False, 1), (592, 64, False, -1))
+POWER = 16
+HEADS = [(dz, other) for dz in (4, 3, 5, 2, 6, 1, 7, 0) for other in (0, 1) if dz or other]
+TOP = 2.0 ** (126 / POWER)
 
 
 def split(value):
@@ -23,6 +26,24 @@
     return high, (value - high.astype(F32)).astype(BF16)
 
 
+def scale_of(value):
+    top = jnp.maximum(jnp.max(jnp.abs(value), axis=0, keepdims=True), 1e-30)
+    return (top * 1.01).astype(BF16).astype(F32)
+
+
+def encode(value, scale):
+    code = jnp.abs(value) * (TOP / scale)
+    for _ in range(4):
+        code = code * code
+    return jnp.where(value < 0, -code, code).astype(BF16)
+
+
+def decode(code, scale):
+    code = code.astype(F32)
+    size = jnp.exp2(jnp.log2(jnp.maximum(jnp.abs(code), 2.0**-126)) * (1 / POWER)) * (scale / TOP)
+    return jnp.where(code < 0, -size, size)
+
+
 def nt(left, right):
     return lax.dot_general(left, right, (((1,), (1,)), ((), ())), preferred_element_type=F32)
 
@@ -33,8 +54,8 @@
 
 def kernel(
     ks, km, vs, vm, qs, qm, ot, zt, st, wm, ow, out_ref,
-    kv, qo, big, wt_in, wt, gat, qa, acc, outs, pt, rsb, fin, fin_rx,
-    loc_sem, swp_send, swp_recv, w_sem, g_send, g_recv, h_send, h_recv, r_send, r_recv, y_send, y_recv,
+    kv, qo, big, wt_in, wt, gat, qa, acc, outs, tx, rx,
+    loc_sem, swp_send, swp_recv, w_sem, g_send, g_recv, h_send, h_recv, r_send, r_recv,
 ):
     party = lax.axis_index("party")
     head = lax.axis_index("head")
@@ -46,8 +67,8 @@
     def at_slot(y, xx):
         return (y % NY) * NX + xx % NX
 
-    def at_z(zz):
-        return {"head": (zz % NZ) * 2 + ylo}
+    def at_head(dz, other):
+        return {"head": ((z + dz) % NZ) * 2 + (1 - ylo if other else ylo)}
 
     peers = [
         sib,
@@ -55,10 +76,7 @@
         {"seq": at_slot(yh, x + NX - 1)},
         {"seq": at_slot(yh + 1, x)},
         {"seq": at_slot(yh + NY - 1, x)},
-        at_z(z + 1),
-        at_z(z + NZ - 1),
-        {"head": z * 2 + 1 - ylo},
-    ]
+    ] + [at_head(dz, other) for dz, other in HEADS]
     barrier = pltpu.get_barrier_semaphore()
     for peer in peers:
         pl.semaphore_signal(barrier, inc=1, device_id=peer, device_id_type=pl.DeviceIdType.MESH)
@@ -96,13 +114,16 @@
     def wide(ref):
         return ref[...].astype(F32)
 
-    kh, kl = split(wide(kv.at[0, 0]) + wide(kv.at[0, 1]))
-    bh, bl = split(wide(kv.at[1, 0]) + wide(kv.at[1, 1]))
-    dh, dl = split(
-        (wide(kv.at[2, 0]) - wide(kv.at[3, 0])) + (wide(kv.at[2, 1]) - wide(kv.at[3, 1]))
-    )
-    for i, value in enumerate((kh, kl, bh, bl, dh, dl, kv[3, 0], kv[3, 1])):
-        gat[seq, i] = value
+    k = wide(kv.at[0, 0]) + wide(kv.at[0, 1])
+    b = wide(kv.at[1, 0]) + wide(kv.at[1, 1])
+    d = (wide(kv.at[2, 0]) - wide(kv.at[3, 0])) + (wide(kv.at[2, 1]) - wide(kv.at[3, 1]))
+    scales = [scale_of(value) for value in (k, b, d)]
+    for i, value in enumerate((k, b, d)):
+        gat[seq, i * T : (i + 1) * T] = encode(value, scales[i])
+    gat[seq, 3 * T : 4 * T] = kv[3, 0]
+    gat[seq, 4 * T : 5 * T] = kv[3, 1]
+    row = lax.broadcasted_iota(jnp.int32, (16, T), 0)
+    gat[seq, SCALES:] = jnp.where(row == 0, scales[0], jnp.where(row == 1, scales[1], scales[2])).astype(BF16)
 
     sends = []
 
@@ -167,7 +188,12 @@
 
     def attend(slot):
         cols = pl.ds(pl.multiple_of(slot * T, T), T)
-        kh, kl, bh, bl, dh, dl, c0, c1 = [gat[slot, i] for i in range(8)]
+        scales = gat[slot, SCALES:].astype(F32)
+        (kh, kl), (bh, bl), (dh, dl) = [
+            split(decode(gat[slot, i * T : (i + 1) * T], scales[i : i + 1])) for i in range(3)
+        ]
+        c0 = gat[slot, 3 * T : 4 * T]
+        c1 = gat[slot, 4 * T : 5 * T]
         scores = nt(qa[...], jnp.concatenate([kh, kl, kh, bh, bl, bh], axis=1))
         zz = big[0, 0, :, cols].astype(F32) + big[0, 1, :, cols].astype(F32)
         sq = big[1, 0, :, cols].astype(F32) + big[1, 1, :, cols].astype(F32)
@@ -193,13 +219,6 @@
     def attend_at(dy, dx):
         attend(at_slot(yh + dy + NY, x + dx + NX))
 
-    attend_at(0, 0)
-    for chunk in range(4):
-        receive(chunk, 1, 0)
-    for chunk in range(4):
-        receive(chunk, 2, 0)
-    for chunk in range(4):
-        receive(chunk, 0, 1)
     weights_in.wait()
 
     @pl.loop(0, 20)
@@ -207,6 +226,13 @@
         cols = pl.ds(pl.multiple_of(i * T, T), T)
         wt[cols, :] = wt_in[:, cols].T
 
+    attend_at(0, 0)
+    for chunk in range(4):
+        receive(chunk, 1, 0)
+    for chunk in range(4):
+        receive(chunk, 2, 0)
+    for chunk in range(4):
+        receive(chunk, 0, 1)
     for chunk in range(4):
         receive(chunk, 0, 2)
     for dy, dx in ((1, 0), (-1, 0), (0, 1), (0, -1)):
@@ -247,65 +273,34 @@
     oh, ol = split(jnp.concatenate([outs[0], outs[1]], axis=1))
     ohl = jnp.concatenate([oh, ol], axis=1)
 
-    def project(zz):
-        rows = pl.ds(pl.multiple_of((zz % NZ) * 2 * COLS, 2 * COLS), 2 * COLS)
-        part = wt[rows, :]
-        pt[zz % NZ] = nt(jnp.concatenate([part, part], axis=1), ohl)
-
-    ring = []
-
-    def ring_copy(way, step, sub, src):
-        index = (way * (NZ - 1) + step) * SUBS + sub
-        return pltpu.make_async_remote_copy(
-            src_ref=src,
-            dst_ref=rsb.at[way, step, pl.ds(sub * ROWS, ROWS)],
-            send_sem=r_send.at[index],
-            recv_sem=r_recv.at[index],
-            device_id=at_z(z + 1) if way == 0 else at_z(z + NZ - 1),
-            device_id_type=pl.DeviceIdType.MESH,
-        )
-
-    def block_of(way, step):
-        return (z - 1 - step + 2 * NZ) % NZ if way == 0 else (z + 1 + step) % NZ
-
-    def local(way, step, sub):
-        return pt.at[block_of(way, step), pl.ds(way * COLS + sub * ROWS, ROWS)]
-
-    project(z + NZ - 1)
-    for sub in range(SUBS):
-        ring.append(ring_copy(0, 0, sub, local(0, 0, sub)))
-        ring[-1].start()
-    project(z + 1)
-    for sub in range(SUBS):
-        ring.append(ring_copy(1, 0, sub, local(1, 0, sub)))
-        ring[-1].start()
-    for step in (2, 6, 3, 5, 4, 0):
-        project(z + step)
-    for step in range(1, NZ):
-        for sub in range(SUBS):
-            for way in range(2):
-                index = ring_copy(way, step - 1, sub, local(way, 0, sub))
-                index.wait_recv()
-                place = rsb.at[way, step - 1, pl.ds(sub * ROWS, ROWS)]
-                total = place[...] + local(way, step, sub)[...]
-                if step < NZ - 1:
-                    place[...] = total
-                    ring.append(ring_copy(way, step, sub, place))
-                    ring[-1].start()
-                else:
-                    fin[way, pl.ds(sub * ROWS, ROWS)] = total
-    last = pltpu.make_async_remote_copy(
-        src_ref=fin.at[1 - ylo],
-        dst_ref=fin_rx,
-        send_sem=y_send,
-        recv_sem=y_recv,
-        device_id={"head": z * 2 + 1 - ylo},
-        device_id_type=pl.DeviceIdType.MESH,
-    )
-    last.start()
-    last.wait_recv()
-    out_ref[...] = fin[ylo] + fin_rx[...]
-    for one in swaps + sends + [swap] + ring + [last]:
+    def project(dz, other):
+        target = ((z + dz) % NZ) * 2 + (1 - ylo if other else ylo)
+        part = wt[pl.ds(pl.multiple_of(target * COLS, COLS), COLS), :]
+        return nt(jnp.concatenate([part, part], axis=1), ohl)
+
+    out_sends = []
+    for i, (dz, other) in enumerate(HEADS):
+        value = project(dz, other)
+        scale = scale_of(value)
+        tx[i, :COLS] = encode(value, scale)
+        tx[i, COLS:] = jnp.broadcast_to(scale, (16, T)).astype(BF16)
+        out_sends.append(
+            pltpu.make_async_remote_copy(
+                src_ref=tx.at[i],
+                dst_ref=rx.at[i],
+                send_sem=r_send.at[i],
+                recv_sem=r_recv.at[i],
+                device_id=at_head(dz, other),
+                device_id_type=pl.DeviceIdType.MESH,
+            )
+        )
+        out_sends[-1].start()
+    total = project(0, 0)
+    for i, one in enumerate(out_sends):
+        one.wait_recv()
+        total += decode(rx[i, :COLS], rx[i, COLS:][:1].astype(F32))
+    out_ref[...] = total
+    for one in swaps + sends + [swap] + out_sends:
         one.wait_send()
 
 
@@ -325,14 +320,12 @@
             pltpu.VMEM((3, 2, T, SLOTS * T), BF16),
             pltpu.VMEM((2 * T, 16 * COLS), BF16),
             pltpu.VMEM((16 * COLS, 2 * T), BF16),
-            pltpu.VMEM((SLOTS, 8, T, T), BF16),
+            pltpu.VMEM((SLOTS, BLOCK, T), BF16),
             pltpu.VMEM((T, 6 * T), BF16),
             pltpu.VMEM((2, T, T), F32),
             pltpu.VMEM((2, T, T), F32),
-            pltpu.VMEM((NZ, 2 * COLS, T), F32),
-            pltpu.VMEM((2, NZ - 1, COLS, T), F32),
-            pltpu.VMEM((2, COLS, T), F32),
-            pltpu.VMEM((COLS, T), F32),
+            pltpu.VMEM((len(HEADS), COLS + 16, T), BF16),
+            pltpu.VMEM((len(HEADS), COLS + 16, T), BF16),
             dma((10,)),
             dma((10,)),
             dma((10,)),
@@ -341,13 +334,11 @@
             dma((64,)),
             dma,
             dma,
-            dma((2 * (NZ - 1) * SUBS,)),
-            dma((2 * (NZ - 1) * SUBS,)),
-            dma,
-            dma,
+            dma((len(HEADS),)),
+            dma((len(HEADS),)),
         ],
         compiler_params=pltpu.CompilerParams(
-            collective_id=0, has_side_effects=True, vmem_limit_bytes=40 * 1024 * 1024
+            collective_id=0, has_side_effects=True, vmem_limit_bytes=60 * 1024 * 1024
         ),
     )(
         key_share, key_mask, value_share, value_mask, query_share, query_mask, output_triple,

time: 92.8 us -> 68.3 us (0.74)
  the two profiles are of different devices: /device:TPU:8 before, /device:TPU:1 now
where the time goes in v2:
time: 68.3 us; the launch traced here: 68.2 us
  Pallas kernels  66.6 us (98%)
  local copies, waits for them, and re-layouts  1.53 us (2%)
    pallas_call x1, Pallas kernels, body(): pl.pallas_call(kernel, out_shape=jax.ShapeDtypeStruct((COLS, T), F32), in...  66.6 us
    unnamed x1, local copies, waits for them, and re-layouts  1.53 us

profile of v2, /device:TPU:1, one launch (start us, length us, event | category | flops | bytes accessed | tf_op | source)
XLA Modules:
  0.0 68.2 jit_solution(10473316243002321467)
XLA Ops:
  0.0 66.6 %shard_map.109 = f32[160,128]{1,0:T(8,128)} custom-call(bf16[1,2,128,128]{3,2,1,0:T(8,128)(2,1)} %ks.1, bf16[1,2,128,128]{3,2,1,0:T(8,128)(2,1)} %km.1, bf16[1,2,128,128]{3,2,1,0:T(8,128)(2,1)} %vs.1, bf16[1,2,128,128]{3,2,1,0:T(8,128)(2,1)} %vm.1, bf16[1,2,128,128]{3,2,1,0:T(8,128)(2,1)} %qs.1, bf16[1,2,128,128]{3,2,1,0:T(8,128)(2,1)} %qm.1, ...), custom_call_target="tpu_custom_call" | custom-call | tf_op jit(solution)/shard_map/pallas_call | solution.py:312
  66.6 1.5 %copy.13 = f32[1,128,160]{1,2,0:T(8,128)} copy(f32[1,128,160]{1,2,0:T(8,128)} %bitcast.3) | data formatting | bytes 163840

commit v3 on v2

--- a/solution.py
+++ b/solution.py
@@ -17,7 +17,7 @@
 BLOCK = SCALES + 16
 CHUNKS = ((0, 256, True, 1), (256, 256, True, -1), (512, 80, False, 1), (592, 64, False, -1))
 POWER = 16
-HEADS = [(dz, other) for dz in (4, 3, 5, 2, 6, 1, 7, 0) for other in (0, 1) if dz or other]
+STEPS = (4, 3, 5, 2, 6, 1, 7, 0)
 TOP = 2.0 ** (126 / POWER)
 
 
@@ -54,8 +54,8 @@
 
 def kernel(
     ks, km, vs, vm, qs, qm, ot, zt, st, wm, ow, out_ref,
-    kv, qo, big, wt_in, wt, gat, qa, acc, outs, tx, rx,
-    loc_sem, swp_send, swp_recv, w_sem, g_send, g_recv, h_send, h_recv, r_send, r_recv,
+    kv, qo, big, wt_in, wt, gat, qa, acc, outs, ty, ry, tz, rz,
+    loc_sem, swp_send, swp_recv, w_sem, g_send, g_recv, h_send, h_recv, y_send, y_recv, z_send, z_recv, round_1, round_2,
 ):
     party = lax.axis_index("party")
     head = lax.axis_index("head")
@@ -67,19 +67,27 @@
     def at_slot(y, xx):
         return (y % NY) * NX + xx % NX
 
-    def at_head(dz, other):
-        return {"head": ((z + dz) % NZ) * 2 + (1 - ylo if other else ylo)}
-
+    def at_z(dz):
+        return {"head": ((z + dz) % NZ) * 2 + ylo}
+
+    pair = {"head": z * 2 + 1 - ylo}
     peers = [
         sib,
         {"seq": at_slot(yh, x + 1)},
         {"seq": at_slot(yh, x + NX - 1)},
         {"seq": at_slot(yh + 1, x)},
         {"seq": at_slot(yh + NY - 1, x)},
-    ] + [at_head(dz, other) for dz, other in HEADS]
+        at_z(1),
+        at_z(NZ - 1),
+        pair,
+    ]
+
+    def tell(semaphore, peer):
+        pl.semaphore_signal(semaphore, inc=1, device_id=peer, device_id_type=pl.DeviceIdType.MESH)
+
     barrier = pltpu.get_barrier_semaphore()
     for peer in peers:
-        pl.semaphore_signal(barrier, inc=1, device_id=peer, device_id_type=pl.DeviceIdType.MESH)
+        tell(barrier, peer)
 
     arrays = [ks, km, vs, vm, qs, qm, ot, zt, st, wm]
     places = [kv.at[i] for i in range(4)] + [qo.at[i] for i in range(3)] + [big.at[i] for i in range(3)]
@@ -104,26 +112,15 @@
         )
         swaps[-1].start()
 
+    tell(round_1, at_z(1))
+    tell(round_1, at_z(NZ - 1))
+
     def arrived(i):
         locals_[i].wait()
         swaps[i].wait_recv()
 
-    for i in range(4):
-        arrived(i)
-
     def wide(ref):
         return ref[...].astype(F32)
-
-    k = wide(kv.at[0, 0]) + wide(kv.at[0, 1])
-    b = wide(kv.at[1, 0]) + wide(kv.at[1, 1])
-    d = (wide(kv.at[2, 0]) - wide(kv.at[3, 0])) + (wide(kv.at[2, 1]) - wide(kv.at[3, 1]))
-    scales = [scale_of(value) for value in (k, b, d)]
-    for i, value in enumerate((k, b, d)):
-        gat[seq, i * T : (i + 1) * T] = encode(value, scales[i])
-    gat[seq, 3 * T : 4 * T] = kv[3, 0]
-    gat[seq, 4 * T : 5 * T] = kv[3, 1]
-    row = lax.broadcasted_iota(jnp.int32, (16, T), 0)
-    gat[seq, SCALES:] = jnp.where(row == 0, scales[0], jnp.where(row == 1, scales[1], scales[2])).astype(BF16)
 
     sends = []
 
@@ -157,7 +154,12 @@
         send(chunk, first, 1, y, xx, not y_first, sign)
         send(chunk, first, 2, y, xx, not y_first, -sign)
 
+    received = set()
+
     def receive(chunk, first, second):
+        if (chunk, first, second) in received or first == second == 0:
+            return
+        received.add((chunk, first, second))
         _, _, y_first, sign = CHUNKS[chunk]
         y, xx = origin(chunk, first, second)
         copy(chunk, first, second, y, xx, seq).wait_recv()
@@ -168,11 +170,36 @@
         elif second == 1:
             send(chunk, first, 3, y, xx, not y_first, sign)
 
-    for chunk, (_, _, y_first, sign) in enumerate(CHUNKS):
-        send(chunk, 1, 0, yh, x, y_first, sign)
-        send(chunk, 2, 0, yh, x, y_first, -sign)
-    for chunk in range(4):
-        spread_second(chunk, 0)
+    def spread_first(chunk, first):
+        _, _, y_first, sign = CHUNKS[chunk]
+        send(chunk, first, 0, yh, x, y_first, sign if first == 1 else -sign)
+
+    scales = []
+
+    def place(i, value):
+        scales.append(scale_of(value))
+        gat[seq, i * T : (i + 1) * T] = encode(value, scales[i])
+
+    arrived(0)
+    arrived(1)
+    place(0, wide(kv.at[0, 0]) + wide(kv.at[0, 1]))
+    place(1, wide(kv.at[1, 0]) + wide(kv.at[1, 1]))
+    spread_first(0, 1)
+    spread_first(0, 2)
+    spread_second(0, 0)
+    arrived(2)
+    arrived(3)
+    place(2, (wide(kv.at[2, 0]) - wide(kv.at[3, 0])) + (wide(kv.at[2, 1]) - wide(kv.at[3, 1])))
+    gat[seq, 3 * T : 4 * T] = kv[3, 0]
+    spread_first(1, 1)
+    spread_first(1, 2)
+    spread_second(1, 0)
+    gat[seq, 4 * T : 5 * T] = kv[3, 1]
+    row = lax.broadcasted_iota(jnp.int32, (16, T), 0)
+    gat[seq, SCALES:] = jnp.where(row == 0, scales[0], jnp.where(row == 1, scales[1], scales[2])).astype(BF16)
+    for chunk in (2, 3):
+        spread_first(chunk, 1)
+        spread_first(chunk, 2)
 
     for i in range(4, 7):
         arrived(i)
@@ -217,6 +244,10 @@
         )
 
     def attend_at(dy, dx):
+        for chunk, (_, _, y_first, sign) in enumerate(CHUNKS):
+            moves = (0, -sign, sign, 2)
+            first, second = (dy, dx) if y_first else (dx, dy)
+            receive(chunk, moves.index(first), moves.index(second))
         attend(at_slot(yh + dy + NY, x + dx + NX))
 
     weights_in.wait()
@@ -226,38 +257,42 @@
         cols = pl.ds(pl.multiple_of(i * T, T), T)
         wt[cols, :] = wt_in[:, cols].T
 
+    def receive_all(chunks, first, second):
+        for chunk in chunks:
+            receive(chunk, first, second)
+
+    AB, CD = (0, 1), (2, 3)
+    receive_all(AB, 0, 1)
+    receive_all(AB, 1, 0)
+    receive_all(AB, 2, 0)
+    for chunk in CD:
+        spread_second(chunk, 0)
+    receive_all(CD, 1, 0)
+    receive_all(CD, 2, 0)
+    pl.semaphore_wait(round_1, 2)
+    tell(round_2, at_z(2))
+    tell(round_2, at_z(NZ - 2))
     attend_at(0, 0)
-    for chunk in range(4):
-        receive(chunk, 1, 0)
-    for chunk in range(4):
-        receive(chunk, 2, 0)
-    for chunk in range(4):
-        receive(chunk, 0, 1)
-    for chunk in range(4):
-        receive(chunk, 0, 2)
-    for dy, dx in ((1, 0), (-1, 0), (0, 1), (0, -1)):
+    receive_all(AB, 1, 1)
+    receive_all(AB, 2, 1)
+    receive_all(AB, 3, 0)
+    receive_all(CD, 0, 1)
+    receive_all(CD, 3, 0)
+    attend_at(0, 1)
+    attend_at(0, -1)
+    receive_all(CD, 1, 1)
+    receive_all(CD, 2, 1)
+    receive_all(AB, 3, 1)
+    attend_at(1, 0)
+    attend_at(-1, 0)
+    receive_all(CD, 3, 1)
+    attend_at(0, 2)
+    attend_at(2, 0)
+    for dy, dx in ((1, 1), (1, -1), (-1, 1), (-1, -1)):
         attend_at(dy, dx)
-    for chunk in range(4):
-        receive(chunk, 3, 0)
-    for chunk in range(4):
-        receive(chunk, 1, 1)
-        receive(chunk, 2, 1)
-    for chunk in range(4):
-        receive(chunk, 0, 3)
-        receive(chunk, 1, 2)
-        receive(chunk, 2, 2)
-        receive(chunk, 3, 1)
-    for dy, dx in ((2, 0), (0, 2), (1, 1), (1, -1), (-1, 1), (-1, -1)):
+    pl.semaphore_wait(round_2, 2)
+    for dy, dx in ((1, 2), (-1, 2), (2, 1), (2, -1), (2, 2)):
         attend_at(dy, dx)
-    for chunk in range(4):
-        receive(chunk, 3, 2)
-        receive(chunk, 1, 3)
-        receive(chunk, 2, 3)
-    for dy, dx in ((2, 1), (2, -1), (1, 2), (-1, 2)):
-        attend_at(dy, dx)
-    for chunk in range(4):
-        receive(chunk, 3, 3)
-    attend_at(2, 2)
 
     swap = pltpu.make_async_remote_copy(
         src_ref=acc.at[1 - party],
@@ -273,33 +308,47 @@
     oh, ol = split(jnp.concatenate([outs[0], outs[1]], axis=1))
     ohl = jnp.concatenate([oh, ol], axis=1)
 
-    def project(dz, other):
-        target = ((z + dz) % NZ) * 2 + (1 - ylo if other else ylo)
+    def project(dz, column):
+        target = ((z + dz) % NZ) * 2 + column
         part = wt[pl.ds(pl.multiple_of(target * COLS, COLS), COLS), :]
         return nt(jnp.concatenate([part, part], axis=1), ohl)
 
     out_sends = []
-    for i, (dz, other) in enumerate(HEADS):
-        value = project(dz, other)
+
+    def pass_on(value, i, src, dst, sends_sem, recvs_sem, peer):
         scale = scale_of(value)
-        tx[i, :COLS] = encode(value, scale)
-        tx[i, COLS:] = jnp.broadcast_to(scale, (16, T)).astype(BF16)
+        src[i, :COLS] = encode(value, scale)
+        src[i, COLS:] = jnp.broadcast_to(scale, (16, T)).astype(BF16)
         out_sends.append(
             pltpu.make_async_remote_copy(
-                src_ref=tx.at[i],
-                dst_ref=rx.at[i],
-                send_sem=r_send.at[i],
-                recv_sem=r_recv.at[i],
-                device_id=at_head(dz, other),
+                src_ref=src.at[i],
+                dst_ref=dst.at[i],
+                send_sem=sends_sem.at[i],
+                recv_sem=recvs_sem.at[i],
+                device_id=peer,
                 device_id_type=pl.DeviceIdType.MESH,
             )
         )
         out_sends[-1].start()
-    total = project(0, 0)
-    for i, one in enumerate(out_sends):
+        return out_sends[-1]
+
+    def incoming(ref, i):
+        return decode(ref[i, :COLS], ref[i, COLS:][:1].astype(F32))
+
+    from_pair = [
+        pass_on(project(dz, 1 - ylo), i, ty, ry, y_send, y_recv, pair) for i, dz in enumerate(STEPS)
+    ]
+    from_z = []
+    for i, dz in enumerate(STEPS):
+        value = project(dz, ylo)
+        from_pair[i].wait_recv()
+        value += incoming(ry, i)
+        if dz:
+            from_z.append(pass_on(value, i, tz, rz, z_send, z_recv, at_z(dz)))
+    for i, one in enumerate(from_z):
         one.wait_recv()
-        total += decode(rx[i, :COLS], rx[i, COLS:][:1].astype(F32))
-    out_ref[...] = total
+        value += incoming(rz, i)
+    out_ref[...] = value
     for one in swaps + sends + [swap] + out_sends:
         one.wait_send()
 
@@ -324,8 +373,10 @@
             pltpu.VMEM((T, 6 * T), BF16),
             pltpu.VMEM((2, T, T), F32),
             pltpu.VMEM((2, T, T), F32),
-            pltpu.VMEM((len(HEADS), COLS + 16, T), BF16),
-            pltpu.VMEM((len(HEADS), COLS + 16, T), BF16),
+            pltpu.VMEM((NZ, COLS + 16, T), BF16),
+            pltpu.VMEM((NZ, COLS + 16, T), BF16),
+            pltpu.VMEM((NZ - 1, COLS + 16, T), BF16),
+            pltpu.VMEM((NZ - 1, COLS + 16, T), BF16),
             dma((10,)),
             dma((10,)),
             dma((10,)),
@@ -334,8 +385,12 @@
             dma((64,)),
             dma,
             dma,
-            dma((len(HEADS),)),
-            dma((len(HEADS),)),
+            dma((NZ,)),
+            dma((NZ,)),
+            dma((NZ - 1,)),
+            dma((NZ - 1,)),
+            pltpu.SemaphoreType.REGULAR,
+            pltpu.SemaphoreType.REGULAR,
         ],
         compiler_params=pltpu.CompilerParams(
             collective_id=0, has_side_effects=True, vmem_limit_bytes=60 * 1024 * 1024

time: 68.3 us -> 61 us (0.89)
  Pallas kernels: 66.6 us -> 59.4 us
    pallas_call x1, Pallas kernels: 66.6 us -> 59.4 us  [body(): pl.pallas_call(kernel, out_shape=jax.ShapeDtypeStruct((COLS, T), F32), in...]
where the time goes in v3:
time: 61 us; the launch traced here: 60.9 us
  Pallas kernels  59.4 us (97%)
  local copies, waits for them, and re-layouts  1.53 us (3%)
    pallas_call x1, Pallas kernels, body(): pl.pallas_call(kernel, out_shape=jax.ShapeDtypeStruct((COLS, T), F32), in...  59.4 us
    unnamed x1, local copies, waits for them, and re-layouts  1.53 us

profile of v3, /device:TPU:1, one launch (start us, length us, event | category | flops | bytes accessed | tf_op | source)
XLA Modules:
  0.0 60.9 jit_solution(9242555746364522328)
XLA Ops:
  0.0 59.4 %shard_map.109 = f32[160,128]{1,0:T(8,128)} custom-call(bf16[1,2,128,128]{3,2,1,0:T(8,128)(2,1)} %ks.1, bf16[1,2,128,128]{3,2,1,0:T(8,128)(2,1)} %km.1, bf16[1,2,128,128]{3,2,1,0:T(8,128)(2,1)} %vs.1, bf16[1,2,128,128]{3,2,1,0:T(8,128)(2,1)} %vm.1, bf16[1,2,128,128]{3,2,1,0:T(8,128)(2,1)} %qs.1, bf16[1,2,128,128]{3,2,1,0:T(8,128)(2,1)} %qm.1, ...), custom_call_target="tpu_custom_call" | custom-call | tf_op jit(solution)/shard_map/pallas_call | solution.py:361
  59.4 1.5 %copy.13 = f32[1,128,160]{1,2,0:T(8,128)} copy(f32[1,128,160]{1,2,0:T(8,128)} %bitcast.3) | data formatting | bytes 163840

commit v4 on v3

v4 whole, which is shorter than its diff:
```python
import functools

import jax
import jax.numpy as jnp
from jax import lax
from jax.experimental import pallas as pl
from jax.experimental.pallas import tpu as pltpu
from jax.sharding import PartitionSpec as P

F32 = jnp.float32
BF16 = jnp.bfloat16
T = 128
NX, NY, NZ = 4, 4, 8
SLOTS = NX * NY
REL = {0: 0, -1: 1, 1: 2, 2: 3, -2: 3}
COLS = 160
K, B, SCALES, D, C0, C1 = 0, T, 2 * T, 2 * T + 16, 3 * T + 16, 4 * T + 16
BLOCK = 5 * T + 16
CHUNKS = ((0, 272, True, 1), (272, 272, True, -1), (544, 64, False, 1), (608, 48, False, -1))
ORDER = (
    ("y", 0, -1),
    ("y", 1, 1),
    ("x", 3, 1),
    ("yx", 0, 0, -1),
    ("yx", 1, 0, 1),
    ("x", 2, 1),
    ("x", 3, -1),
    ("x", 2, -1),
    ("x", 3, 2),
    ("y", 1, -1),
    ("yx", 1, 0, -1),
    ("yx", 0, 0, 1),
    ("y", 0, 1),
    ("yx", 0, 0, 2),
    ("x", 2, 2),
    ("yx", 1, 0, 2),
    ("y", 1, 2),
    ("yx", 0, -1, 1),
    ("y", 0, 2),
    ("yx", 1, 1, -1),
    ("yx", 1, 1, 1),
    ("yx", 0, -1, -1),
    ("turn",),
    ("yx", 1, -1, 1),
    ("xy", 3, "rest", 1),
    ("yx", 0, 1, -1),
    ("xy", 2, "own", -1),
    ("xy", 2, "rest", -1),
    ("query",),
    ("yx", 0, 1, 1),
    ("yx", 1, -1, -1),
    ("xy", 3, "own", 1),
    ("attend", 0, 1),
    ("xy", 2, "rest", 1),
    ("yx", 1, 1, 2),
    ("yx", 0, 2, -1),
    ("xy", 3, "own", -1),
    ("attend", 0, -1),
    ("xy", 3, "rest", -1),
    ("attend", 0, 2),
    ("yx", 0, 1, 2),
    ("yx", 1, 2, 1),
    ("attend", 0, 0),
    ("xy", 2, "own", 1),
    ("yx", 1, 2, -1),
    ("xy", 2, "own", 2),
    ("xy", 3, "own", 2),
    ("yx", 1, -1, 2),
    ("xy", 2, "rest", 2),
    ("xy", 3, "rest", 2),
    ("yx", 0, -1, 2),
    ("attend", -1, 0),
    ("yx", 0, 2, 1),
    ("attend", 1, -1),
    ("yx", 0, 2, 2),
    ("attend", 1, 1),
    ("attend", -1, -1),
    ("yx", 1, 2, 2),
    ("attend", 2, 0),
    ("attend", 1, 2),
    ("attend", -1, 1),
    ("attend", 1, 0),
    ("attend", 2, 1),
    ("attend", 2, -1),
    ("attend", -1, 2),
    ("attend", 2, 2),
)
GROUPS = {"all": (0, 4), "own": (0, 1), "rest": (1, 3)}
SPLIT = {0: "own", 1: "rest", -1: "rest", 2: "rest"}
MESSAGES = sum(entry[0] in ("y", "x", "yx", "xy") for entry in ORDER)
POWER = 16
STEPS = (4, 3, 5, 2, 6, 1, 7, 0)
TOP = 2.0 ** (126 / POWER)


def split(value):
    high = value.astype(BF16)
    return high, (value - high.astype(F32)).astype(BF16)


def scale_of(value):
    top = jnp.maximum(jnp.max(jnp.abs(value), axis=0, keepdims=True), 1e-30)
    return (top * 1.01).astype(BF16).astype(F32)


def encode(value, scale):
    code = jnp.abs(value) * (TOP / scale)
    for _ in range(4):
        code = code * code
    return jnp.where(value < 0, -code, code).astype(BF16)


def decode(code, scale):
    code = code.astype(F32)
    size = jnp.exp2(jnp.log2(jnp.maximum(jnp.abs(code), 2.0**-126)) * (1 / POWER)) * (scale / TOP)
    return jnp.where(code < 0, -size, size)


def nt(left, right):
    return lax.dot_general(left, right, (((1,), (1,)), ((), ())), preferred_element_type=F32)


def nn(left, right):
    return lax.dot_general(left, right, (((1,), (0,)), ((), ())), preferred_element_type=F32)


def kernel(
    ks, km, vs, vm, qs, qm, ot, zt, st, wm, ow, out_ref,
    kv, qo, big, wt_in, wt, gat, qa, acc, outs, ty, ry, tz, rz,
    loc_sem, swp_send, swp_recv, w_sem, g_send, g_recv, h_send, h_recv, y_send, y_recv, z_send, z_recv, round_1, round_2,
):
    party = lax.axis_index("party")
    head = lax.axis_index("head")
    seq = lax.axis_index("seq")
    z, ylo = head // 2, head % 2
    yh, x = seq // NX, seq % NX
    xs = {step: lax.rem(x + step + NX, NX) for step in (0, 1, -1, 2)}
    ys = {step: lax.rem(yh + step + NY, NY) for step in (0, 1, -1, 2)}
    zs = {step: lax.rem(z + step, NZ) * 2 for step in range(NZ)}
    sib = (1 - party, head, seq)
    pair = (party, z * 2 + 1 - ylo, seq)
    along_x = {step: (party, head, yh * NX + xs[step]) for step in (1, -1)}
    along_y = {step: (party, head, ys[step] * NX + x) for step in (1, -1)}
    along_z = {step: (party, zs[step] + ylo, seq) for step in range(1, NZ)}
    peers = [
        sib, along_x[1], along_x[-1], along_y[1], along_y[-1], along_z[1], along_z[NZ - 1], pair
    ]

    def tell(semaphore, peer):
        pl.semaphore_signal(semaphore, inc=1, device_id=peer, device_id_type=pl.DeviceIdType.MESH)

    barrier = pltpu.get_barrier_semaphore()
    for peer in peers:
        tell(barrier, peer)

    arrays = [ks, km, vs, vm, qs, qm, ot, zt, st, wm]
    places = [kv.at[i] for i in range(4)] + [qo.at[i] for i in range(3)] + [big.at[i] for i in range(3)]
    locals_ = [
        pltpu.make_async_copy(src.at[0, party], dst.at[party], loc_sem.at[i])
        for i, (src, dst) in enumerate(zip(arrays, places))
    ]
    swaps = [
        pltpu.make_async_remote_copy(
            src_ref=src.at[0, 1 - party],
            dst_ref=dst.at[party],
            send_sem=swp_send.at[i],
            recv_sem=swp_recv.at[i],
            device_id=sib,
            device_id_type=pl.DeviceIdType.MESH,
        )
        for i, (src, dst) in enumerate(zip(arrays, places))
    ]
    weights_in = pltpu.make_async_copy(ow, wt_in, w_sem)
    for one in locals_[:4]:
        one.start()
    pl.semaphore_wait(barrier, len(peers))
    for one in swaps[:4]:
        one.start()

    tell(round_1, along_z[1])
    tell(round_1, along_z[NZ - 1])

    def arrived(i):
        locals_[i].wait()
        swaps[i].wait_recv()

    def wide(ref):
        return ref[...].astype(F32)

    sends = []
    copies = {}

    def message(key, chunk, y_axis, step, y_blocks, x_blocks):
        start, count = CHUNKS[chunk][:2]
        (y0, ny), (x0, nx) = y_blocks, x_blocks
        src = gat.at[pl.ds(REL[y0] if ny == 1 else y0, ny), pl.ds(REL[x0] if nx == 1 else x0, nx), pl.ds(start, count)]
        if y_axis:
            y0 = y0 - step
        else:
            x0 = x0 - step
        dst = gat.at[pl.ds(REL[y0] if ny == 1 else y0, ny), pl.ds(REL[x0] if nx == 1 else x0, nx), pl.ds(start, count)]
        index = len(copies)
        copies[key] = pltpu.make_async_remote_copy(
            src_ref=src,
            dst_ref=dst,
            send_sem=g_send.at[index],
            recv_sem=g_recv.at[index],
            device_id=along_y[step] if y_axis else along_x[step],
            device_id_type=pl.DeviceIdType.MESH,
        )
        copies[key].start()
        sends.append(copies[key])

    def deliver(key, chunk, y_axis, others, away):
        sign = CHUNKS[chunk][3]
        step = -sign if away == sign else sign
        block = (-sign if away == 2 else 0, 1)
        message(key, chunk, y_axis, step, *((block, others) if y_axis else (others, block)))

    received = set()

    def receive(*key):
        if key in received:
            return
        received.add(key)
        copies[key].wait_recv()

    scales = []

    def place(i, value):
        scales.append(scale_of(value))
        gat[0, 0, i : i + T] = encode(value, scales[-1])

    for i in range(4):
        arrived(i)
    place(K, wide(kv.at[0, 0]) + wide(kv.at[0, 1]))
    place(B, wide(kv.at[1, 0]) + wide(kv.at[1, 1]))
    place(D, (wide(kv.at[2, 0]) - wide(kv.at[3, 0])) + (wide(kv.at[2, 1]) - wide(kv.at[3, 1])))
    row = lax.broadcasted_iota(jnp.int32, (16, T), 0)
    gat[0, 0, SCALES:D] = jnp.where(row == 0, scales[0], jnp.where(row == 1, scales[1], scales[2])).astype(BF16)
    gat[0, 0, C0:C1] = kv[3, 0]
    gat[0, 0, C1:] = kv[3, 1]

    def others_in():
        weights_in.start()
        for one in locals_[4:] + swaps[4:]:
            one.start()

    def attend(dy, dx):
        slot = ys[dy] * NX + xs[dx]
        ry, rx = REL[dy], REL[dx]
        cols = pl.ds(pl.multiple_of(slot * T, T), T)
        scales = gat[ry, rx, SCALES:D].astype(F32)
        (kh, kl), (bh, bl), (dh, dl) = [
            split(decode(gat[ry, rx, start : start + T], scales[i : i + 1]))
            for i, start in enumerate((K, B, D))
        ]
        c0 = gat[ry, rx, C0:C1]
        c1 = gat[ry, rx, C1:]
        scores = nt(qa[...], jnp.concatenate([kh, kl, kh, bh, bl, bh], axis=1))
        zz = big[0, 0, :, cols].astype(F32) + big[0, 1, :, cols].astype(F32)
        sq = big[1, 0, :, cols].astype(F32) + big[1, 1, :, cols].astype(F32)
        w0 = big[2, 0, :, cols]
        w1 = big[2, 1, :, cols]
        poly = 1.25 + zz + 0.25 * sq + scores * (1.0 + 0.5 * zz + 0.25 * scores)
        row = seq * T + lax.broadcasted_iota(jnp.int32, (T, T), 0)
        col = slot * T + lax.broadcasted_iota(jnp.int32, (T, T), 1)
        weights = jnp.where(col <= row, poly * lax.rsqrt((row + 1).astype(F32)), 0.0)
        lead = weights - w1.astype(F32)
        opened = lead - w0.astype(F32)
        lh, ll = split(lead)
        oh, ol = split(opened)
        both = jnp.concatenate([c0, c1], axis=1)
        mixed = nn(jnp.concatenate([oh, ol], axis=1), jnp.concatenate([both, both], axis=0))
        acc[0] += mixed[:, :T] + nn(
            jnp.concatenate([lh, ll, lh], axis=1), jnp.concatenate([dh, dh, dl], axis=0)
        )
        acc[1] += mixed[:, T:] + nn(
            jnp.concatenate([w1, w1], axis=1), jnp.concatenate([dh, dl], axis=0)
        )

    def prepare():
        for i in range(4, 7):
            arrived(i)
        scale = T ** (-0.5)
        qh, ql = split(scale * (wide(qo.at[0, 0]) + wide(qo.at[0, 1])))
        ah, al = split(-scale * (wide(qo.at[1, 0]) + wide(qo.at[1, 1])))
        for i, value in enumerate((qh, qh, ql, ah, ah, al)):
            qa[:, i * T : (i + 1) * T] = value
        acc[0] = wide(qo.at[2, 0])
        acc[1] = wide(qo.at[2, 1])
        for i in range(7, 10):
            arrived(i)

    def turn():
        weights_in.wait()

        @pl.loop(0, 20)
        def _(i):
            cols = pl.ds(pl.multiple_of(i * T, T), T)
            wt[cols, :] = wt_in[:, cols].T

    def needed(entry):
        kind, rest = entry[0], entry[1:]
        if kind in ("y", "x"):
            chunk, away = rest
            if away == 2:
                receive(kind, chunk, -CHUNKS[chunk][3])
            deliver(entry, chunk, kind == "y", (0, 1), away)
        elif kind in ("yx", "xy"):
            chunk, group, away = rest
            if away == 2:
                receive(kind, chunk, group, -CHUNKS[chunk][3])
            else:
                for first in {"all": (1, -1, 2), "own": (), "rest": (1, -1, 2)}.get(group, (group,) if group else ()):
                    receive(kind[0], chunk, first)
            deliver(entry, chunk, kind == "xy", GROUPS[group] if kind == "xy" else (group, 1), away)
        elif kind == "turn":
            turn()
        elif kind == "query":
            prepare()
        else:
            dy, dx = rest
            for chunk, (_, _, y_first, _) in enumerate(CHUNKS):
                first, second = (dy, dx) if y_first else (dx, dy)
                if second:
                    group = first if y_first else SPLIT[first]
                    receive("yx" if y_first else "xy", chunk, group, second)
                elif first:
                    receive("y" if y_first else "x", chunk, first)
            attend(dy, dx)

    for position, entry in enumerate(ORDER):
        needed(entry)
        if position == 9:
            others_in()
        if position == len(ORDER) // 2:
            pl.semaphore_wait(round_1, 2)
            tell(round_2, along_z[2])
            tell(round_2, along_z[NZ - 2])
        if position == len(ORDER) * 9 // 10:
            pl.semaphore_wait(round_2, 2)

    swap = pltpu.make_async_remote_copy(
        src_ref=acc.at[1 - party],
        dst_ref=outs.at[party],
        send_sem=h_send,
        recv_sem=h_recv,
        device_id=sib,
        device_id_type=pl.DeviceIdType.MESH,
    )
    swap.start()
    outs[party] = acc[party]
    swap.wait_recv()
    oh, ol = split(jnp.concatenate([outs[0], outs[1]], axis=1))
    ohl = jnp.concatenate([oh, ol], axis=1)

    def project(dz, column):
        target = zs[dz] + column
        part = wt[pl.ds(pl.multiple_of(target * COLS, COLS), COLS), :]
        return nt(jnp.concatenate([part, part], axis=1), ohl)

    out_sends = []

    def pass_on(value, i, src, dst, sends_sem, recvs_sem, peer):
        scale = scale_of(value)
        src[i, :COLS] = encode(value, scale)
        src[i, COLS:] = jnp.broadcast_to(scale, (16, T)).astype(BF16)
        out_sends.append(
            pltpu.make_async_remote_copy(
                src_ref=src.at[i],
                dst_ref=dst.at[i],
                send_sem=sends_sem.at[i],
                recv_sem=recvs_sem.at[i],
                device_id=peer,
                device_id_type=pl.DeviceIdType.MESH,
            )
        )
        out_sends[-1].start()
        return out_sends[-1]

    def incoming(ref, i):
        return decode(ref[i, :COLS], ref[i, COLS:][:1].astype(F32))

    from_pair = [
        pass_on(project(dz, 1 - ylo), i, ty, ry, y_send, y_recv, pair) for i, dz in enumerate(STEPS)
    ]
    for one in swaps + sends + [swap]:
        one.wait_send()
    from_z = []
    for i, dz in enumerate(STEPS):
        value = project(dz, ylo)
        from_pair[i].wait_recv()
        value += incoming(ry, i)
        if dz:
            from_z.append(pass_on(value, i, tz, rz, z_send, z_recv, along_z[dz]))
    for i, one in enumerate(from_z):
        one.wait_recv()
        value += incoming(rz, i)
    out_ref[...] = value
    for one in out_sends:
        one.wait_send()


def body(
    query_share, key_share, value_share, query_mask, key_mask, value_mask,
    score_triple, square_triple, weight_mask, output_triple, out_weight,
):
    dma = pltpu.SemaphoreType.DMA
    result = pl.pallas_call(
        kernel,
        out_shape=jax.ShapeDtypeStruct((COLS, T), F32),
        in_specs=[pl.BlockSpec(memory_space=pl.ANY)] * 11,
        out_specs=pl.BlockSpec(memory_space=pltpu.VMEM),
        scratch_shapes=[
            pltpu.VMEM((4, 2, T, T), BF16),
            pltpu.VMEM((3, 2, T, T), BF16),
            pltpu.VMEM((3, 2, T, SLOTS * T), BF16),
            pltpu.VMEM((2 * T, 16 * COLS), BF16),
            pltpu.VMEM((16 * COLS, 2 * T), BF16),
            pltpu.VMEM((NY, NX, BLOCK, T), BF16),
            pltpu.VMEM((T, 6 * T), BF16),
            pltpu.VMEM((2, T, T), F32),
            pltpu.VMEM((2, T, T), F32),
            pltpu.VMEM((NZ, COLS + 16, T), BF16),
            pltpu.VMEM((NZ, COLS + 16, T), BF16),
            pltpu.VMEM((NZ - 1, COLS + 16, T), BF16),
            pltpu.VMEM((NZ - 1, COLS + 16, T), BF16),
            dma((10,)),
            dma((10,)),
            dma((10,)),
            dma,
            dma((MESSAGES,)),
            dma((MESSAGES,)),
            dma,
            dma,
            dma((NZ,)),
            dma((NZ,)),
            dma((NZ - 1,)),
            dma((NZ - 1,)),
            pltpu.SemaphoreType.REGULAR,
            pltpu.SemaphoreType.REGULAR,
        ],
        compiler_params=pltpu.CompilerParams(
            collective_id=0, has_side_effects=True, vmem_limit_bytes=60 * 1024 * 1024
        ),
    )(
        key_share, key_mask, value_share, value_mask, query_share, query_mask, output_triple,
        score_triple, square_triple, weight_mask, out_weight,
    )
    return result.T[None]


def solution(mesh):
    shares = P("party", "head", "seq", None)
    return jax.shard_map(
        body,
        mesh=mesh,
        in_specs=(shares,) * 10 + (P("head", None),),
        out_specs=P("party", "seq", "head"),
        check_vma=False,
    )
```

time: 61 us -> 57.6 us (0.944)
  Pallas kernels: 59.4 us -> 55.9 us
    pallas_call x1, Pallas kernels: 59.4 us -> 55.9 us  [body(): pl.pallas_call(kernel, out_shape=jax.ShapeDtypeStruct((COLS, T), F32), in...]
where the time goes in v4:
time: 57.6 us; the launch traced here: 57.4 us
  Pallas kernels  55.9 us (97%)
  local copies, waits for them, and re-layouts  1.53 us (3%)
    pallas_call x1, Pallas kernels, body(): pl.pallas_call(kernel, out_shape=jax.ShapeDtypeStruct((COLS, T), F32), in...  55.9 us
    unnamed x1, local copies, waits for them, and re-layouts  1.53 us

profile of v4, /device:TPU:1, one launch (start us, length us, event | category | flops | bytes accessed | tf_op | source)
XLA Modules:
  0.0 57.4 jit_solution(11670551254326163375)
XLA Ops:
  0.0 55.9 %shard_map.109 = f32[160,128]{1,0:T(8,128)} custom-call(bf16[1,2,128,128]{3,2,1,0:T(8,128)(2,1)} %ks.1, bf16[1,2,128,128]{3,2,1,0:T(8,128)(2,1)} %km.1, bf16[1,2,128,128]{3,2,1,0:T(8,128)(2,1)} %vs.1, bf16[1,2,128,128]{3,2,1,0:T(8,128)(2,1)} %vm.1, bf16[1,2,128,128]{3,2,1,0:T(8,128)(2,1)} %qs.1, bf16[1,2,128,128]{3,2,1,0:T(8,128)(2,1)} %qm.1, ...), custom_call_target="tpu_custom_call" | custom-call | tf_op jit(solution)/shard_map/pallas_call | solution.py:410
  55.9 1.5 %copy.13 = f32[1,128,160]{1,2,0:T(8,128)} copy(f32[1,128,160]{1,2,0:T(8,128)} %bitcast.3) | data formatting | bytes 163840

commit v5 on v4

--- a/solution.py
+++ b/solution.py
@@ -353,12 +353,13 @@
     outs[party] = acc[party]
     swap.wait_recv()
     oh, ol = split(jnp.concatenate([outs[0], outs[1]], axis=1))
-    ohl = jnp.concatenate([oh, ol], axis=1)
+    ohl = jnp.concatenate([oh, ol], axis=0)
 
     def project(dz, column):
         target = zs[dz] + column
         part = wt[pl.ds(pl.multiple_of(target * COLS, COLS), COLS), :]
-        return nt(jnp.concatenate([part, part], axis=1), ohl)
+        both = nt(part, ohl)
+        return both[:, :T] + both[:, T:]
 
     out_sends = []
 
@@ -385,8 +386,6 @@
     from_pair = [
         pass_on(project(dz, 1 - ylo), i, ty, ry, y_send, y_recv, pair) for i, dz in enumerate(STEPS)
     ]
-    for one in swaps + sends + [swap]:
-        one.wait_send()
     from_z = []
     for i, dz in enumerate(STEPS):
         value = project(dz, ylo)
@@ -394,6 +393,8 @@
         value += incoming(ry, i)
         if dz:
             from_z.append(pass_on(value, i, tz, rz, z_send, z_recv, along_z[dz]))
+    for one in swaps + sends + [swap]:
+        one.wait_send()
     for i, one in enumerate(from_z):
         one.wait_recv()
         value += incoming(rz, i)

time: 57.6 us -> 57.2 us (level)
  no operation moved by 1% of the time
where the time goes in v5:
time: 57.2 us; the launch traced here: 57 us
  Pallas kernels  55.4 us (97%)
  local copies, waits for them, and re-layouts  1.53 us (3%)
    pallas_call x1, Pallas kernels, body(): pl.pallas_call(kernel, out_shape=jax.ShapeDtypeStruct((COLS, T), F32), in...  55.4 us
    unnamed x1, local copies, waits for them, and re-layouts  1.53 us

profile of v5, /device:TPU:1, one launch (start us, length us, event | category | flops | bytes accessed | tf_op | source)
XLA Modules:
  0.0 57.0 jit_solution(10300626353454297271)
XLA Ops:
  0.0 55.4 %shard_map.109 = f32[160,128]{1,0:T(8,128)} custom-call(bf16[1,2,128,128]{3,2,1,0:T(8,128)(2,1)} %ks.1, bf16[1,2,128,128]{3,2,1,0:T(8,128)(2,1)} %km.1, bf16[1,2,128,128]{3,2,1,0:T(8,128)(2,1)} %vs.1, bf16[1,2,128,128]{3,2,1,0:T(8,128)(2,1)} %vm.1, bf16[1,2,128,128]{3,2,1,0:T(8,128)(2,1)} %qs.1, bf16[1,2,128,128]{3,2,1,0:T(8,128)(2,1)} %qm.1, ...), custom_call_target="tpu_custom_call" | custom-call | tf_op jit(solution)/shard_map/pallas_call | solution.py:411
  55.4 1.5 %copy.13 = f32[1,128,160]{1,2,0:T(8,128)} copy(f32[1,128,160]{1,2,0:T(8,128)} %bitcast.3) | data formatting | bytes 163840
